TPU v7x, 1024 devices: a whole 4x8x16 slice. The times are simulated.
1024 devices in a mesh: gx: 16 (over z), gy: 16 (over y, core), gz: 4 (over x).
Axes of the slice: x: 4, y: 8, z: 16, core: 2. Of those that a mesh axis runs over, the one named last changes fastest.
Arguments:
- rhs_local: float32 [24576, 128], P(('gx', 'gy', 'gz')), may hold values from -46 to 46
- geom_diag: float32 [3, 24576, 128], P(None, ('gx', 'gy', 'gz')), may hold values from 0.01 to 0.05
- geom_off: float32 [3, 24576, 128], P(None, ('gx', 'gy', 'gz')), may hold values from -0.0048 to 0.0048
- mass_coef: float32 [24576, 128], P(('gx', 'gy', 'gz')), may hold values from 0.25 to 2.5
- elem_counts: int32 [1024], P(('gx', 'gy', 'gz')), may hold values from 2 to 6, as said below
Outputs:
- solution_nodes: float32 [22528, 120], P(('gx', 'gy', 'gz'))
- residual_nodes: float32 [22528, 120], P(('gx', 'gy', 'gz'))
Inputs may be any that keep to these rules, and one draw needn't show every extreme that they name: `elem_counts`: every partition holds whole layers of 1 x 2 elements; partitions with the same gx index hold the same count, and their widths along gx, in elements, sum to 2 times the number of gx indices.
All inputs are finite; a program needn't handle non-finite values.
Results may differ from a plain program's by a relative error of at most 0.0003.
Values sent between devices are 32-bit elements; how exact they have to be, the bound alone decides.
A program may use at most 32 MiB of HBM per device.

v0:
```python
import jax
import jax.numpy as jnp
import numpy as np
from jax import lax
from jax.sharding import PartitionSpec as P

ORDER = 7
EY = 1
EZ = 2
ITERS = 2


points_gll = (
    -1.0,
    -0.8717401485096066,
    -0.5917001814331423,
    -0.2092992179024789,
    0.2092992179024789,
    0.5917001814331423,
    0.8717401485096066,
    1.0,
)


def extended(x, sides, width):
    for axis, dim in sides:
        peers, length = (lax.axis_size(axis), x.shape[dim])
        up = [(i, (i + 1) % peers) for i in range(peers - 1)]
        down = [(j, i) for i, j in up]
        last = lax.slice_in_dim(x, length - width, length, axis=dim)
        initial = lax.slice_in_dim(x, 0, width, axis=dim)
        before = lax.ppermute(last, axis, up)
        after = lax.ppermute(initial, axis, down)
        x = jnp.concatenate([before, x, after], axis=dim)
    return x


def derivative_table():
    points = np.array(points_gll)
    total_points = points.shape[0]
    weights = np.ones(total_points)
    for j in range(total_points):
        for k in range(total_points):
            if k != j:
                weights[j] = weights[j] / (points[j] - points[k])
    deriv_table = np.zeros((total_points, total_points))
    for i in range(total_points):
        for j in range(total_points):
            if i != j:
                deriv_table[i, j] = weights[j] / weights[i] / (points[i] - points[j])
        deriv_table[i, i] = -np.sum(deriv_table[i])
    return deriv_table


def split_axis(grid_vals, which_axis, elements):
    head_part = lax.slice_in_dim(grid_vals, 0, ORDER * elements, axis=which_axis)
    head_part = head_part.reshape(
        grid_vals.shape[:which_axis] + (elements, ORDER) + grid_vals.shape[which_axis + 1 :]
    )
    tail_part = lax.slice_in_dim(
        grid_vals, ORDER, ORDER * elements + 1, stride=ORDER, axis=which_axis
    )
    return jnp.concatenate(
        [head_part, jnp.expand_dims(tail_part, which_axis + 1)], axis=which_axis + 1
    )


def merge_axis(blocks, which_axis, elements):
    flat_shape = blocks.shape[:which_axis] + (ORDER * elements,) + blocks.shape[which_axis + 2 :]
    head_part = lax.slice_in_dim(blocks, 0, ORDER, axis=which_axis + 1).reshape(flat_shape)
    tail_part = lax.slice_in_dim(blocks, ORDER, ORDER + 1, axis=which_axis + 1)
    zero_shape = list(tail_part.shape)
    zero_shape[which_axis + 1] = ORDER - 1
    tail_part = jnp.concatenate(
        [jnp.zeros(tuple(zero_shape), blocks.dtype), tail_part], axis=which_axis + 1
    )
    tail_part = tail_part.reshape(flat_shape)
    pad_head = [(0, 0)] * len(flat_shape)
    pad_tail = [(0, 0)] * len(flat_shape)
    pad_head[which_axis] = (0, 1)
    pad_tail[which_axis] = (1, 0)
    return jnp.pad(head_part, pad_head) + jnp.pad(tail_part, pad_tail)


def to_elements(grid_vals, slot_count):
    span_y = (grid_vals.shape[1] - 1) // ORDER
    span_z = (grid_vals.shape[2] - 1) // ORDER
    return split_axis(split_axis(split_axis(grid_vals, 0, slot_count), 2, span_y), 4, span_z)


def to_grid(blocks):
    return merge_axis(
        merge_axis(merge_axis(blocks, 4, blocks.shape[4]), 2, blocks.shape[2]), 0, blocks.shape[0]
    )


def element_apply(grid_vals, diag_part, off_part, mass_part, live_slots, deriv_table):
    slot_count = live_slots.shape[0]
    element_vals = to_elements(grid_vals, slot_count)
    block_shape = element_vals.shape
    highest = lax.Precision.HIGHEST
    grad_r = jnp.einsum("ai,xiyjzk->xayjzk", deriv_table, element_vals, precision=highest)
    grad_s = jnp.einsum("bj,xiyjzk->xiybzk", deriv_table, element_vals, precision=highest)
    grad_t = jnp.einsum("ck,xiyjzk->xiyjzc", deriv_table, element_vals, precision=highest)
    g_rr = diag_part[0].reshape(block_shape)
    g_ss = diag_part[1].reshape(block_shape)
    g_tt = diag_part[2].reshape(block_shape)
    g_rs = off_part[0].reshape(block_shape)
    g_rt = off_part[1].reshape(block_shape)
    g_st = off_part[2].reshape(block_shape)
    flux_r = g_rr * grad_r + g_rs * grad_s + g_rt * grad_t
    flux_s = g_rs * grad_r + g_ss * grad_s + g_st * grad_t
    flux_t = g_rt * grad_r + g_st * grad_s + g_tt * grad_t
    result = jnp.einsum("ai,xayjzk->xiyjzk", deriv_table, flux_r, precision=highest)
    result = result + jnp.einsum("bj,xiybzk->xiyjzk", deriv_table, flux_s, precision=highest)
    result = result + jnp.einsum("ck,xiyjzc->xiyjzk", deriv_table, flux_t, precision=highest)
    result = result + mass_part.reshape(block_shape) * element_vals
    result = result * live_slots.reshape(slot_count, 1, 1, 1, 1, 1)
    return to_grid(result)


def region(offsets, last_index, full_shape):
    starts = []
    extents = []
    for which_axis in range(3):
        if offsets[which_axis] == 0:
            starts.append(jnp.int32(0))
            extents.append(full_shape[which_axis])
        elif offsets[which_axis] < 0:
            starts.append(jnp.int32(0))
            extents.append(1)
        else:
            starts.append(jnp.asarray(last_index[which_axis], jnp.int32))
            extents.append(1)
    return (tuple(starts), tuple(extents))


def exchange_direct(grid_vals, last_row):
    full_shape = grid_vals.shape
    slab_len = max(
        full_shape[1] * full_shape[2], full_shape[0] * full_shape[2], full_shape[0] * full_shape[1]
    )
    last_index = (last_row, full_shape[1] - 1, full_shape[2] - 1)
    directions = [
        (step_x, step_y, step_z)
        for step_x in (-1, 0, 1)
        for step_y in (-1, 0, 1)
        for step_z in (-1, 0, 1)
    ]
    outgoing = []
    for offsets in directions:
        if offsets == (0, 0, 0):
            outgoing.append(jnp.zeros((slab_len,), grid_vals.dtype))
        else:
            starts, extents = region(offsets, last_index, full_shape)
            send_piece = lax.dynamic_slice(grid_vals, starts, extents).reshape(-1)
            outgoing.append(jnp.pad(send_piece, (0, slab_len - send_piece.shape[0])))
    sending = jnp.stack(outgoing).reshape(3, 3, 3, slab_len)
    received = extended(sending, (("gx", 0), ("gy", 1), ("gz", 2)), 1)
    for offsets in directions:
        if offsets != (0, 0, 0):
            starts, extents = region(offsets, last_index, full_shape)
            size_piece = extents[0] * extents[1] * extents[2]
            incoming = received[
                2 + 2 * offsets[0], 2 + 2 * offsets[1], 2 + 2 * offsets[2], :size_piece
            ]
            current = lax.dynamic_slice(grid_vals, starts, extents)
            grid_vals = lax.dynamic_update_slice(
                grid_vals, current + incoming.reshape(extents), starts
            )
    return grid_vals


def local(rhs_local, geom_diag, geom_off, mass_coef, elem_counts):
    deriv_table = jnp.asarray(derivative_table(), jnp.float32)
    slot_count = rhs_local.shape[0] // (ORDER + 1)
    x_width = elem_counts[0] // (EY * EZ)
    last_row = ORDER * x_width
    live_slots = (jnp.arange(slot_count) < x_width).astype(jnp.float32)
    block_shape = (slot_count, ORDER + 1, EY, ORDER + 1, EZ, ORDER + 1)
    rows_x = ORDER * slot_count + 1
    rows_y = ORDER * EY + 1
    rows_z = ORDER * EZ + 1

    def assemble(grid_vals):
        return exchange_direct(grid_vals, last_row)

    index_x = lax.axis_index("gx")
    index_y = lax.axis_index("gy")
    index_z = lax.axis_index("gz")
    plane_x = jnp.arange(rows_x)[:, None, None]
    plane_y = jnp.arange(rows_y)[None, :, None]
    plane_z = jnp.arange(rows_z)[None, None, :]
    owner_mask = ((plane_x > 0) | (index_x == 0)) & (plane_x <= last_row)
    owner_mask = owner_mask & ((plane_y > 0) | (index_y == 0)) & ((plane_z > 0) | (index_z == 0))
    owner_mask = owner_mask.astype(jnp.float32)

    def squares(vector):
        return lax.psum(jnp.sum(owner_mask * vector * vector), ("gx", "gy", "gz"))

    rhs_blocks = rhs_local.reshape(block_shape) * live_slots.reshape(slot_count, 1, 1, 1, 1, 1)
    rhs_field = assemble(to_grid(rhs_blocks))
    solution = jnp.zeros_like(rhs_field)
    residual = rhs_field
    direction = rhs_field
    norm_now = squares(residual)
    for step in range(ITERS):
        image_vals = assemble(
            element_apply(direction, geom_diag, geom_off, mass_coef, live_slots, deriv_table)
        )
        curvature = lax.psum(jnp.sum(owner_mask * direction * image_vals), ("gx", "gy", "gz"))
        step_len = norm_now / curvature
        solution = solution + step_len * direction
        residual = residual - step_len * image_vals
        if step + 1 < ITERS:
            norm_next = squares(residual)
            direction = residual + norm_next / norm_now * direction
            norm_now = norm_next
    return (solution.reshape(rows_x, rows_y * rows_z), residual.reshape(rows_x, rows_y * rows_z))


def solution(mesh):
    placed = (
        P(("gx", "gy", "gz"), None),
        P(None, ("gx", "gy", "gz"), None),
        P(None, ("gx", "gy", "gz"), None),
        P(("gx", "gy", "gz"), None),
        P(("gx", "gy", "gz")),
    )
    return jax.shard_map(
        local,
        mesh=mesh,
        in_specs=placed,
        out_specs=(P(("gx", "gy", "gz"), None), P(("gx", "gy", "gz"), None)),
        check_vma=False,
    )
```

profile of v0, /device:TPU:1, one launch (start us, length us, event | category | flops | bytes accessed | tf_op | source)
XLA Modules:
  0.0 575.8 jit_solution(9847486691268647621)
XLA Ops:
  17.0 5.5 collective-permute-start
  30.2 4.0 collective-permute-start.2
  34.2 12.4 %collective-permute-start.3 = (f32[5,1,3,330]{3,2,1,0:T(4,128)S(1)}, f32[5,1,3,330]{3,2,1,0:T(4,128)S(1)}, u32[]{:S(2)}, u32[]{:S(2)}) collective-permute-start(f32[5,1,3,330]{3,2,1,0:T(4,128)S(1)} %get-tuple-element.77), channel_id=1, source_target_pairs={{4,0},{8,4},{12,8},{16,12},{20,16},{24,20},{28,24},{32,28},{36,32}... | collective-permute-start | bytes 59408 | tf_op jit(solution)/shard_map/ppermute | solution.py:33
  60.6 1.7 dynamic_update_slice.245
  62.9 1.7 dynamic_update_slice.247
  65.2 1.7 dynamic_update_slice.250
  94.8 4.0 collective-permute-start.6
  99.8 1.9 collective-permute-start.8
  101.8 3.8 collective-permute-start.9
  107.1 2.9 collective-permute-start.10
  121.8 1.7 dynamic_update_slice.271
  124.1 1.7 dynamic_update_slice.273
  126.4 1.7 dynamic_update_slice.276
  137.1 128.6 %all-reduce.99 = (f32[]{:T(128)}, f32[]{:T(128)}) all-reduce(f32[]{:T(128)} %get-tuple-element.39, f32[]{:T(128)} %get-tuple-element.38), channel_id=1, replica_groups=mesh['gx'=16,'gy'=16,'gz'=4] {'gx','gy','gz'}, use_global_device_ids=true, to_apply=%region_1.2 | all-reduce | flops 2 | bytes 16 | tf_op jit(solution)/shard_map/psum | solution.py:199
  267.8 120.4 %psum.30 = f32[]{:T(128)} all-reduce(f32[]{:T(128)} %fusion.49), channel_id=1, replica_groups=mesh['gx'=16,'gy'=16,'gz'=4] {'gx','gy','gz'}, use_global_device_ids=true, to_apply=%region_5.6 | all-reduce | flops 1 | bytes 8 | tf_op jit(solution)/shard_map/psum | solution.py:199
  408.4 4.0 collective-permute-start.12
  413.4 3.8 collective-permute-start.14
  417.2 1.9 collective-permute-start.15
  419.3 3.1 collective-permute-done.15
  422.4 3.0 collective-permute-start.16
  437.3 1.7 dynamic_update_slice.297
  439.5 1.7 dynamic_update_slice.299
  441.8 1.7 dynamic_update_slice.302
  452.5 120.6 %psum.31 = f32[]{:T(128)} all-reduce(f32[]{:T(128)} %fusion.51), channel_id=1, replica_groups=mesh['gx'=16,'gy'=16,'gz'=4] {'gx','gy','gz'}, use_global_device_ids=true, to_apply=%region_7.8 | all-reduce | flops 1 | bytes 8 | tf_op jit(solution)/shard_map/psum | solution.py:211
  (585 shorter events, 89.2 us)
Async XLA Ops:
  1.3 0.7 copy-start.3
  10.3 19.8 %collective-permute-start.1 = (f32[1,3,3,330]{3,2,1,0:T(4,128)S(1)}, f32[1,3,3,330]{3,2,1,0:T(4,128)S(1)}, u32[]{:S(2)}, u32[]{:S(2)}) collective-permute-start(f32[1,3,3,330]{3,2,1,0:T(4,128)S(1)} %slice.438), channel_id=1, source_target_pairs={{64,0},{128,64},{192,128},{256,192},{320,256},{384,320},{448,384},... | collective-permute-start | bytes 35648 | tf_op jit(solution)/shard_map/ppermute | solution.py:33
  17.0 13.1 %collective-permute-start = (f32[1,3,3,330]{3,2,1,0:T(4,128)S(1)}, f32[1,3,3,330]{3,2,1,0:T(4,128)S(1)}, u32[]{:S(2)}, u32[]{:S(2)}) collective-permute-start(f32[1,3,3,330]{3,2,1,0:T(4,128)S(1)} %slice.437), channel_id=1, source_target_pairs={{0,64},{64,128},{128,192},{192,256},{256,320},{320,384},{384,448},... | collective-permute-start | bytes 35648 | tf_op jit(solution)/shard_map/ppermute | solution.py:32
  22.7 0.8 copy-start.1
  24.8 0.8 copy-start.2
  28.9 0.7 copy-start.4
  30.2 16.7 %collective-permute-start.2 = (f32[5,1,3,330]{3,2,1,0:T(4,128)S(1)}, f32[5,1,3,330]{3,2,1,0:T(4,128)S(1)}, u32[]{:S(2)}, u32[]{:S(2)}) collective-permute-start(f32[5,1,3,330]{3,2,1,0:T(4,128)S(1)} %get-tuple-element.76), channel_id=1, source_target_pairs={{0,4},{4,8},{8,12},{12,16},{16,20},{20,24},{24,28},{28,32},{32,36}... | collective-permute-start | bytes 59408 | tf_op jit(solution)/shard_map/ppermute | solution.py:32
  34.2 13.2 %collective-permute-start.3 = (f32[5,1,3,330]{3,2,1,0:T(4,128)S(1)}, f32[5,1,3,330]{3,2,1,0:T(4,128)S(1)}, u32[]{:S(2)}, u32[]{:S(2)}) collective-permute-start(f32[5,1,3,330]{3,2,1,0:T(4,128)S(1)} %get-tuple-element.77), channel_id=1, source_target_pairs={{4,0},{8,4},{12,8},{16,12},{20,16},{24,20},{28,24},{32,28},{36,32}... | collective-permute-start | bytes 59408 | tf_op jit(solution)/shard_map/ppermute | solution.py:33
  47.6 2.9 collective-permute-start.4
  48.9 4.7 collective-permute-start.5
  76.5 0.7 copy-start
  87.8 12.0 %collective-permute-start.7 = (f32[1,3,3,330]{3,2,1,0:T(4,128)S(1)}, f32[1,3,3,330]{3,2,1,0:T(4,128)S(1)}, u32[]{:S(2)}, u32[]{:S(2)}) collective-permute-start(f32[1,3,3,330]{3,2,1,0:T(4,128)S(1)} %slice.488), channel_id=1, source_target_pairs={{64,0},{128,64},{192,128},{256,192},{320,256},{384,320},{448,384},... | collective-permute-start | bytes 35648 | tf_op jit(solution)/shard_map/ppermute | solution.py:33
  94.8 4.9 collective-permute-start.6
  99.8 6.0 %collective-permute-start.8 = (f32[5,1,3,330]{3,2,1,0:T(4,128)S(1)}, f32[5,1,3,330]{3,2,1,0:T(4,128)S(1)}, u32[]{:S(2)}, u32[]{:S(2)}) collective-permute-start(f32[5,1,3,330]{3,2,1,0:T(4,128)S(1)} %get-tuple-element.74), channel_id=1, source_target_pairs={{0,4},{4,8},{8,12},{12,16},{16,20},{20,24},{24,28},{28,32},{32,36}... | collective-permute-start | bytes 59408 | tf_op jit(solution)/shard_map/ppermute | solution.py:32
  101.8 5.2 collective-permute-start.9
  107.1 4.4 collective-permute-start.10
  109.9 4.8 collective-permute-start.11
  401.3 12.1 %collective-permute-start.13 = (f32[1,3,3,330]{3,2,1,0:T(4,128)S(1)}, f32[1,3,3,330]{3,2,1,0:T(4,128)S(1)}, u32[]{:S(2)}, u32[]{:S(2)}) collective-permute-start(f32[1,3,3,330]{3,2,1,0:T(4,128)S(1)} %slice.532), channel_id=1, source_target_pairs={{64,0},{128,64},{192,128},{256,192},{320,256},{384,320},{448,384},... | collective-permute-start | bytes 35648 | tf_op jit(solution)/shard_map/ppermute | solution.py:33
  408.4 4.9 collective-permute-start.12
  413.4 5.9 %collective-permute-start.14 = (f32[5,1,3,330]{3,2,1,0:T(4,128)S(1)}, f32[5,1,3,330]{3,2,1,0:T(4,128)S(1)}, u32[]{:S(2)}, u32[]{:S(2)}) collective-permute-start(f32[5,1,3,330]{3,2,1,0:T(4,128)S(1)} %get-tuple-element.72), channel_id=1, source_target_pairs={{0,4},{4,8},{8,12},{12,16},{16,20},{20,24},{24,28},{28,32},{32,36}... | collective-permute-start | bytes 59408 | tf_op jit(solution)/shard_map/ppermute | solution.py:32
  417.2 5.2 collective-permute-start.15
  422.4 4.6 collective-permute-start.16
  425.5 4.7 collective-permute-start.17
where the time goes:
time: 583 us; the launch traced here: 576 us
  blocking collectives  370 us (63%)
  local copies, waits for them, and re-layouts  62.6 us (11%)
  starting transfers between devices  56.3 us (10%)
  between operations  51.5 us (9%)
  other arithmetic  23.7 us (4%)
  waiting for transfers between devices  8.38 us (1%)
    psum x2, blocking collectives, squares(): return lax.psum(jnp.sum(owner_mask * vector * vector), ('gx', 'gy', 'gz'))  249 us
    psum x1, blocking collectives, local(): lax.psum(jnp.sum(owner_mask * direction * image_vals), ('gx', 'gy', 'gz'))  121 us
    ppermute x9, starting transfers between devices, extended(): before = lax.ppermute(last, axis, up)  30.3 us
    dynamic_update_slice x72, local copies, waits for them, and re-layouts, exchange_direct(): lax.dynamic_update_slice(grid_vals, current + incoming.reshape(extents),...  29.1 us
    ppermute x9, starting transfers between devices, extended(): after = lax.ppermute(initial, axis, down)  25.9 us
    add x60, other arithmetic, exchange_direct(): current + incoming.reshape(extents)  15.9 us
  transfers between devices with their start and end apart: 18, of which 6 were waited for; matrix products, arithmetic and copies ran while one was open for 2% of the time, Pallas kernels for 0%

commit v1 on v0

v1 whole, which is shorter than its diff:
```python
import functools

import jax
import jax.numpy as jnp
import numpy as np
from jax import lax
from jax.experimental import pallas as pl
from jax.experimental.pallas import tpu as pltpu
from jax.sharding import PartitionSpec as P

ORDER = 7
NODES = ORDER + 1
EY = 1
EZ = 2
SLOTS = 3
ROWS = SLOTS * NODES
LANES = EY * NODES * EZ * NODES
PLANES_X = ORDER * SLOTS + 1
PLANES_YZ = (ORDER * EY + 1) * (ORDER * EZ + 1)
AXES = ("gx", "gy", "gz")
MESH = pl.DeviceIdType.MESH
F32 = jnp.float32
BF16 = jnp.bfloat16

points_gll = (
    -1.0,
    -0.8717401485096066,
    -0.5917001814331423,
    -0.2092992179024789,
    0.2092992179024789,
    0.5917001814331423,
    0.8717401485096066,
    1.0,
)

SIDES = ((-1, -1), (-1, 1), (1, -1), (1, 1), (0, -1), (0, 1), (-1, 0), (1, 0), (0, 0))


def derivative_table():
    points = np.array(points_gll)
    total_points = points.shape[0]
    weights = np.ones(total_points)
    for j in range(total_points):
        for k in range(total_points):
            if k != j:
                weights[j] = weights[j] / (points[j] - points[k])
    deriv_table = np.zeros((total_points, total_points))
    for i in range(total_points):
        for j in range(total_points):
            if i != j:
                deriv_table[i, j] = weights[j] / weights[i] / (points[i] - points[j])
        deriv_table[i, i] = -np.sum(deriv_table[i])
    return deriv_table


def tables():
    deriv = derivative_table().astype(np.float32)
    eye8, eye2 = np.eye(NODES, dtype=np.float32), np.eye(EZ, dtype=np.float32)
    along_s = np.kron(deriv, np.kron(eye2, eye8))
    along_t = np.kron(eye8, np.kron(eye2, deriv))
    forward = np.concatenate([along_s.T, along_t.T], axis=1)
    backward = np.concatenate([along_s, along_t], axis=0)

    radial = np.zeros((2 * NODES + 1, NODES, LANES), np.float32)
    for i in range(NODES):
        radial[i] = deriv[:, i][:, None]
        radial[NODES + i] = deriv[i, :][:, None]
    lanes = np.arange(LANES)
    distance = lanes // 16 + (lanes % 16 > 8)
    kept = lanes % 16 != 8
    for bit in range(4):
        for lane in lanes[kept]:
            if distance[lane] >> bit & 1:
                radial[2 * NODES, bit, lane - (distance[lane] & ((2 << bit) - 1))] = 1.0
    return forward, backward, radial


def wrapped(value, step, size):
    return lax.rem(value + (step + size), size)


def kernel(
    sizes,
    counts_ref,
    rhs_hbm,
    diag_hbm,
    off_hbm,
    mass_hbm,
    forward_hbm,
    backward_hbm,
    radial_hbm,
    solution_ref,
    residual_ref,
    rhs_ref,
    diag_ref,
    off_ref,
    mass_ref,
    forward_ref,
    backward_ref,
    forward_terms,
    backward_terms,
    radial_ref,
    outgoing,
    fields,
    edges,
    sums_out,
    sums_in,
    load_sem,
    send_sem,
    field_sem,
    edge_sem,
    sum_send_sem,
    sum_sem,
):
    here = tuple(lax.axis_index(axis) for axis in AXES)
    index_x, index_y, index_z = here

    def at(steps):
        return tuple(
            wrapped(here[i], steps[i], sizes[i]) if steps[i] else here[i] for i in range(3)
        )

    lines = []
    for axis in (0, 1, 2):
        line = []
        for step in range(1, sizes[axis]):
            steps = [0, 0, 0]
            steps[axis] = step
            line.append(tuple(steps))
        lines.append(line)

    partners = {tuple(s % n for s, n in zip(steps, sizes)) for line in lines for steps in line}
    partners |= {
        tuple(s % n for s, n in zip((dx, dy, dz), sizes))
        for dx in (-1, 0, 1)
        for dy, dz in SIDES
        if (dx, dy, dz) != (0, 0, 0)
    }
    partners = sorted(partners)
    barrier = pltpu.get_barrier_semaphore()
    for steps in partners:
        pl.semaphore_signal(barrier, inc=1, device_id=at(steps), device_id_type=MESH)

    loads = [
        pltpu.make_async_copy(source, target, load_sem.at[i])
        for i, (source, target) in enumerate(
            (
                (rhs_hbm, rhs_ref),
                (forward_hbm, forward_ref),
                (radial_hbm, radial_ref),
                (diag_hbm, diag_ref),
                (off_hbm, off_ref),
                (mass_hbm, mass_ref),
                (backward_hbm, backward_ref),
            )
        )
    ]
    for load in loads:
        load.start()

    lane = lax.broadcasted_iota(jnp.int32, (NODES, LANES), 1)
    row = lax.broadcasted_iota(jnp.int32, (NODES, LANES), 0)
    in_group = lane & 15
    zero = jnp.zeros((NODES, LANES), F32)

    keep_z = {
        1: (in_group == 0) & (index_z < sizes[2] - 1),
        -1: (in_group == 15) & (index_z > 0),
    }
    keep_y = {
        1: (lane < 16) & (index_y < sizes[1] - 1),
        -1: (lane >= LANES - 16) & (index_y > 0),
    }
    turn_z = {1: LANES - 15, -1: 15}
    turn_y = {1: 16, -1: LANES - 16}

    def tiled(function, *tiles):
        return [function(*parts) for parts in zip(*tiles)]

    def moved(tiles, turn, keep):
        return [jnp.where(keep, pltpu.roll(t, turn, 1), zero) for t in tiles]

    loads[0].wait()
    width = counts_ref[0] // (EY * EZ)
    live = [width > slot for slot in range(SLOTS)]

    def joined(tiles):
        tiles = [
            t
            + jnp.where(
                in_group == 7,
                pltpu.roll(t, LANES - 1, 1),
                jnp.where(in_group == 8, pltpu.roll(t, 1, 1), zero),
            )
            for t in tiles
        ]
        out = []
        for slot in range(SLOTS):
            total = tiles[slot]
            if slot:
                before = jnp.where(row == 0, pltpu.roll(tiles[slot - 1], 1, 0), zero)
                total = jnp.where(live[slot], total + before, zero)
            if slot + 1 < SLOTS:
                total = total + jnp.where(
                    row == NODES - 1, pltpu.roll(tiles[slot + 1], NODES - 1, 0), zero
                )
            out.append(total)
        return out

    def last_tile(tiles):
        return jnp.where(live[2], tiles[2], jnp.where(live[1], tiles[1], tiles[0]))

    def pack(turn, tiles):
        by_z = {0: tiles}
        for dz in (-1, 1):
            by_z[dz] = moved(tiles, turn_z[dz], keep_z[dz])
        for k, (dy, dz) in enumerate(SIDES):
            message = moved(by_z[dz], turn_y[dy], keep_y[dy]) if dy else by_z[dz]
            for slot in range(SLOTS):
                outgoing[turn, k, pl.ds(slot * NODES, NODES), :] = message[slot]
            outgoing[turn, k, pl.ds(ROWS, NODES), :] = last_tile(message)

    def edge_row(dx, k):
        return (16 if k == 8 else 8 * 0 + k) + ((1 if k == 8 else 8) if dx < 0 else 0)

    def send(turn):
        for k, (dy, dz) in enumerate(SIDES):
            for dx in (-1, 1):
                source = ROWS + NODES - 1 if dx > 0 else 0
                pltpu.make_async_remote_copy(
                    src_ref=outgoing.at[turn, k, pl.ds(source, 1)],
                    dst_ref=edges.at[turn, pl.ds(edge_row(dx, k), 1)],
                    send_sem=send_sem.at[turn, 1],
                    recv_sem=edge_sem.at[turn],
                    device_id=at((dx, dy, dz)),
                    device_id_type=MESH,
                ).start()
            if k < 8:
                pltpu.make_async_remote_copy(
                    src_ref=outgoing.at[turn, k, pl.ds(0, ROWS)],
                    dst_ref=fields.at[turn, pl.ds(k * ROWS, ROWS)],
                    send_sem=send_sem.at[turn, 0],
                    recv_sem=field_sem.at[turn],
                    device_id=at((0, dy, dz)),
                    device_id_type=MESH,
                ).start()

    def wait_bytes(ref, sem):
        pltpu.make_async_copy(ref, ref, sem).wait()

    def receive(turn, tiles):
        wait_bytes(edges.at[turn, pl.ds(0, 18)], edge_sem.at[turn])
        wait_bytes(fields.at[turn], field_sem.at[turn])
        before = jnp.sum(edges[turn, 0:8, :], axis=0, keepdims=True) + edges[turn, 16:17, :]
        after = jnp.sum(edges[turn, 8:16, :], axis=0, keepdims=True) + edges[turn, 17:18, :]
        before = jnp.where((row == 0) & (index_x > 0), before, zero)
        after = jnp.where((row == NODES - 1) & (index_x < sizes[0] - 1), after, zero)
        out = []
        for slot in range(SLOTS):
            parts = [
                fields[turn, pl.ds(k * ROWS + slot * NODES, NODES), :] for k in range(8)
            ]
            total = ((parts[0] + parts[1]) + (parts[2] + parts[3])) + (
                (parts[4] + parts[5]) + (parts[6] + parts[7])
            )
            if slot == 0:
                total = total + before
            is_last = live[slot] & jnp.logical_not(live[slot + 1]) if slot + 1 < SLOTS else live[slot]
            total = total + jnp.where(is_last, after, zero)
            out.append(tiles[slot] + total)
        return out

    def three_terms(values):
        high = values.astype(BF16)
        low = (values - high.astype(F32)).astype(BF16)
        return jnp.concatenate([high, low, high], axis=1)

    def rows_of(tiles):
        return jnp.concatenate(tiles, axis=0)

    def tiles_of(values):
        return [values[slot * NODES : (slot + 1) * NODES, :] for slot in range(SLOTS)]

    def along_r(tiles, first):
        out = []
        for t in tiles:
            terms = [radial_ref[first + i] * t[i : i + 1, :] for i in range(NODES)]
            out.append(
                ((terms[0] + terms[1]) + (terms[2] + terms[3]))
                + ((terms[4] + terms[5]) + (terms[6] + terms[7]))
            )
        return out

    def fluxes(tiles):
        lane_grads = jnp.dot(
            three_terms(rows_of(tiles)), forward_terms[...], preferred_element_type=F32
        )
        grad_r = along_r(tiles, 0)
        grad_s = tiles_of(lane_grads[:, :LANES])
        grad_t = tiles_of(lane_grads[:, LANES:])
        flux = ([], [], [])
        for slot in range(SLOTS):
            at_slot = pl.ds(slot * NODES, NODES)
            g_rr, g_ss, g_tt = (diag_ref[i, at_slot, :] for i in range(3))
            g_rs, g_rt, g_st = (off_ref[i, at_slot, :] for i in range(3))
            u_r, u_s, u_t = grad_r[slot], grad_s[slot], grad_t[slot]
            flux[0].append(g_rr * u_r + g_rs * u_s + g_rt * u_t)
            flux[1].append(g_rs * u_r + g_ss * u_s + g_st * u_t)
            flux[2].append(g_rt * u_r + g_st * u_s + g_tt * u_t)
        return (grad_r, grad_s, grad_t), flux

    def mass_times(tiles):
        return [mass_ref[pl.ds(slot * NODES, NODES), :] * tiles[slot] for slot in range(SLOTS)]

    def image_of(flux, mass_part):
        packed = jnp.concatenate([rows_of(flux[1]), rows_of(flux[2])], axis=1)
        lane_part = tiles_of(
            jnp.dot(three_terms(packed), backward_terms[...], preferred_element_type=F32)
        )
        return tiled(lambda a, b, c: (a + c) + b, lane_part, along_r(flux[0], NODES), mass_part)

    def dot(left, right):
        return (left[0] * right[0] + left[1] * right[1]) + left[2] * right[2]

    raw = [
        jnp.where(live[slot], rhs_ref[pl.ds(slot * NODES, NODES), :], zero)
        for slot in range(SLOTS)
    ]
    base = joined(raw)
    pack(0, base)
    for load in loads[1:]:
        load.wait()
    for matrix, terms in ((forward_ref, forward_terms), (backward_ref, backward_terms)):
        depth = matrix.shape[0]
        values = matrix[...]
        high = values.astype(BF16)
        terms[0:depth, :] = high
        terms[depth : 2 * depth, :] = high
        terms[2 * depth : 3 * depth, :] = (values - high.astype(F32)).astype(BF16)
    pl.semaphore_wait(barrier, len(partners))
    send(0)
    base = receive(0, base)

    unused, flux = fluxes(base)
    first_raw = image_of(flux, mass_times(base))
    first = joined(first_raw)
    pack(1, first)
    send(1)
    moment0 = dot(base, raw)
    moment1 = dot(base, first_raw)
    first = receive(1, first)

    moment2 = dot(first, first_raw)
    grads, flux = fluxes(first)
    mass_part = mass_times(first)
    moment3 = (dot(grads[0], flux[0]) + dot(grads[1], flux[1])) + (
        dot(grads[2], flux[2]) + dot(first, mass_part)
    )

    def halves(a, b):
        low = lane < 64
        return jnp.where(low, a, b) + pltpu.roll(jnp.where(low, b, a), 64, 1)

    odd, even = halves(moment0, moment1), halves(moment2, moment3)
    pairs = jnp.where(
        (lane & 32) != 0,
        odd + pltpu.roll(odd, 32, 1),
        even + pltpu.roll(even, LANES - 32, 1),
    )
    total = jnp.sum(pairs, axis=0, keepdims=True)

    def start_line(axis, value):
        sums_out[axis, 0:1, :] = value
        for k, steps in enumerate(lines[axis]):
            pltpu.make_async_remote_copy(
                src_ref=sums_out.at[axis, pl.ds(0, 1)],
                dst_ref=sums_in.at[axis, pl.ds(k, 1)],
                send_sem=sum_send_sem.at[axis],
                recv_sem=sum_sem.at[axis],
                device_id=at(steps),
                device_id_type=MESH,
            ).start()

    def finish_line(axis, value):
        count = len(lines[axis])
        wait_bytes(sums_in.at[axis, pl.ds(0, count)], sum_sem.at[axis])
        return value + jnp.sum(sums_in[axis, 0:count, :], axis=0, keepdims=True)

    def packed_grid(tiles):
        out = []
        for t in tiles:
            for bit in range(4):
                take = radial_ref[2 * NODES, bit : bit + 1, :] > 0.5
                t = jnp.where(take, pltpu.roll(t, LANES - (1 << bit), 1), t)
            out.append(t)
        return [
            out[0],
            jnp.where(row < NODES - 1, pltpu.roll(out[1], NODES - 1, 0), pltpu.roll(out[2], NODES - 2, 0)),
            pltpu.roll(out[2], NODES - 2, 0),
        ]

    start_line(0, total)
    second = joined(image_of(flux, mass_part))
    pack(2, second)
    send(2)
    base_grid = packed_grid(base)
    first_grid = packed_grid(first)
    total = finish_line(0, total)
    start_line(1, total)
    second_grid = packed_grid(receive(2, second))
    total = finish_line(1, total)
    start_line(2, total)
    total = finish_line(2, total)

    group = lax.broadcasted_iota(jnp.int32, (1, LANES), 1) // 32
    m2, m0, m3, m1 = (
        jnp.sum(jnp.where(group == k, total, 0.0), axis=1, keepdims=True) for k in range(4)
    )
    alpha0 = m0 / m1
    gain = (m2 / m1) * alpha0
    alpha1 = alpha0 * (gain - 1.0) / (alpha0 * (alpha0 * (m3 / m1)) - gain * gain)
    scale0 = alpha0 + alpha1 * gain
    scale1 = alpha0 * alpha1
    for slot in range(SLOTS):
        count = min(NODES, PLANES_X - slot * NODES)
        at_slot = pl.ds(slot * NODES, count)
        iterate = scale0 * base_grid[slot] - scale1 * first_grid[slot]
        rest = base_grid[slot] - scale0 * first_grid[slot] + scale1 * second_grid[slot]
        solution_ref[at_slot, :] = iterate[:count, :PLANES_YZ]
        residual_ref[at_slot, :] = rest[:count, :PLANES_YZ]

    for turn in range(3):
        wait_bytes(edges.at[turn, pl.ds(0, 18)], send_sem.at[turn, 1])
        wait_bytes(fields.at[turn], send_sem.at[turn, 0])
    for axis in range(3):
        wait_bytes(sums_in.at[axis, pl.ds(0, len(lines[axis]))], sum_send_sem.at[axis])


def local(sizes, rhs_local, geom_diag, geom_off, mass_coef, elem_counts):
    forward, backward, radial = tables()
    hbm = pl.BlockSpec(memory_space=pltpu.HBM)
    vmem = pl.BlockSpec(memory_space=pltpu.VMEM)
    out = jax.ShapeDtypeStruct((PLANES_X, PLANES_YZ), F32)
    return pl.pallas_call(
        functools.partial(kernel, sizes),
        name="cg",
        out_shape=(out, out),
        in_specs=[pl.BlockSpec(memory_space=pltpu.SMEM)] + [hbm] * 7,
        out_specs=(vmem, vmem),
        scratch_shapes=[
            pltpu.VMEM((ROWS, LANES), F32),
            pltpu.VMEM((3, ROWS, LANES), F32),
            pltpu.VMEM((3, ROWS, LANES), F32),
            pltpu.VMEM((ROWS, LANES), F32),
            pltpu.VMEM(forward.shape, F32),
            pltpu.VMEM(backward.shape, F32),
            pltpu.VMEM((3 * forward.shape[0], forward.shape[1]), BF16),
            pltpu.VMEM((3 * backward.shape[0], backward.shape[1]), BF16),
            pltpu.VMEM(radial.shape, F32),
            pltpu.VMEM((3, 9, ROWS + NODES, LANES), F32),
            pltpu.VMEM((3, 8 * ROWS, LANES), F32),
            pltpu.VMEM((3, 24, LANES), F32),
            pltpu.VMEM((3, 8, LANES), F32),
            pltpu.VMEM((3, 16, LANES), F32),
            pltpu.SemaphoreType.DMA((7,)),
            pltpu.SemaphoreType.DMA((3, 2)),
            pltpu.SemaphoreType.DMA((3,)),
            pltpu.SemaphoreType.DMA((3,)),
            pltpu.SemaphoreType.DMA((3,)),
            pltpu.SemaphoreType.DMA((3,)),
        ],
        compiler_params=pltpu.CompilerParams(
            collective_id=0, has_side_effects=True, vmem_limit_bytes=16 * 1024 * 1024
        ),
    )(
        elem_counts,
        *(
            pltpu.with_memory_space_constraint(array, pltpu.HBM)
            for array in (
                rhs_local,
                geom_diag,
                geom_off,
                mass_coef,
                jnp.asarray(forward),
                jnp.asarray(backward),
                jnp.asarray(radial),
            )
        ),
    )


def solution(mesh):
    placed = (
        P(AXES, None),
        P(None, AXES, None),
        P(None, AXES, None),
        P(AXES, None),
        P(AXES),
    )
    sizes = tuple(mesh.shape[axis] for axis in AXES)
    return jax.shard_map(
        functools.partial(local, sizes),
        mesh=mesh,
        in_specs=placed,
        out_specs=(P(AXES, None), P(AXES, None)),
        check_vma=False,
    )
```

time: 583 us -> 52.5 us (0.09); the launches traced: 576 us -> 52.3 us
  blocking collectives: 370 us -> 0 us
  local copies, waits for them, and re-layouts: 62.6 us -> 1.2 us
  starting transfers between devices: 56.3 us -> 0 us
  between operations: 51.5 us -> 1.29 us
  Pallas kernels: 0 us -> 49.8 us
  other arithmetic: 23.7 us -> 0 us
  waiting for transfers between devices: 8.38 us -> 0 us
    psum x3 -> x0, blocking collectives: 370 us -> none  [the longest x2 249 us: squares(): return lax.psum(jnp.sum(owner_mask * vector * vector), ('gx', 'gy', 'gz'))]
    ppermute x18 -> x0, starting transfers between devices: 56.3 us -> none  [the longest x9 30.3 us: extended(): before = lax.ppermute(last, axis, up)]
    pallas_call x0 -> x1, Pallas kernels: none -> 49.8 us  [local(): pl.pallas_call(functools.partial(kernel, sizes), name='cg', out_shape=(ou...]
    dynamic_update_slice x72 -> x0, local copies, waits for them, and re-layouts: 29.1 us -> none  [exchange_direct(): lax.dynamic_update_slice(grid_vals, current + incoming.reshape(extents),...]
    add x76 -> x0, other arithmetic: 16.4 us -> none  [the longest x60 15.9 us: exchange_direct(): current + incoming.reshape(extents)]
    another operation x162 -> x0, local copies, waits for them, and re-layouts: 10.2 us -> none  [the longest x54 4.48 us: exchange_direct(): incoming.reshape(extents)]
    dynamic_slice x15 -> x0, local copies, waits for them, and re-layouts: 9.04 us -> none  [the longest x9 5.05 us: exchange_direct(): current = lax.dynamic_slice(grid_vals, starts, extents)]
    ppermute x18 -> x0, waiting for transfers between devices: 8.38 us -> none  [the longest x9 8.36 us: extended(): after = lax.ppermute(initial, axis, down)]
  transfers between devices with their start and end apart: 18 -> 0, of which waited for: 6 -> 0; matrix products, arithmetic and copies ran while one was open for 2% -> 0% of each run, Pallas kernels for 0% -> 0%
where the time goes in v1:
time: 52.5 us; the launch traced here: 52.3 us
  Pallas kernels  49.8 us (95%)
  between operations  1.29 us (2%)
  local copies, waits for them, and re-layouts  1.2 us (2%)
    pallas_call x1, Pallas kernels, local(): pl.pallas_call(functools.partial(kernel, sizes), name='cg', out_shape=(ou...  49.8 us
    unnamed x2, local copies, waits for them, and re-layouts  1.2 us

profile of v1, /device:TPU:1, one launch (start us, length us, event | category | flops | bytes accessed | tf_op | source)
XLA Modules:
  0.0 52.3 jit_solution(12482388843968480232)
XLA Ops:
  1.3 49.8 %cg.1 = (f32[22,120]{1,0:T(8,128)S(1)}, f32[22,120]{1,0:T(8,128)S(1)}) custom-call(s32[1]{0:T(128)S(6)} %copy.12.counts_ref, f32[24,128]{1,0:T(8,128)} %rhs_hbm.1, f32[3,24,128]{2,1,0:T(8,128)} %diag_hbm.1, f32[3,24,128]{2,1,0:T(8,128)} %off_hbm.1, f32[24,128]{1,0:T(8,128)} %mass_hbm.1, f32[128,256]{1,0:T(8,128)} %constant.6.clone.forward_hbm, ...), custom_call_target="tpu_custom_call" | custom-call | tf_op jit(solution)/shard_map/cg/pallas_call | solution.py:444
  51.1 0.6 %copy.13 = f32[22,120]{1,0:T(8,128)} copy(f32[22,120]{1,0:T(8,128)S(1)} %get-tuple-element.4) | data formatting | bytes 21120
  51.7 0.6 %copy.14 = f32[22,120]{1,0:T(8,128)} copy(f32[22,120]{1,0:T(8,128)S(1)} %get-tuple-element.5) | data formatting | bytes 21120

commit v2 on v1

--- a/solution.py
+++ b/solution.py
@@ -34,6 +34,10 @@
 )
 
 SIDES = ((-1, -1), (-1, 1), (1, -1), (1, 1), (0, -1), (0, 1), (-1, 0), (1, 0), (0, 0))
+NEIGHBOURS = sorted(
+    ((dx, dy, dz) for dx in (-1, 0, 1) for dy, dz in SIDES if (dx, dy, dz) != (0, 0, 0)),
+    key=lambda steps: -sum(map(abs, steps)),
+)
 
 
 def derivative_table():
@@ -75,10 +79,6 @@
     return forward, backward, radial
 
 
-def wrapped(value, step, size):
-    return lax.rem(value + (step + size), size)
-
-
 def kernel(
     sizes,
     counts_ref,
@@ -89,8 +89,7 @@
     forward_hbm,
     backward_hbm,
     radial_hbm,
-    solution_ref,
-    residual_ref,
+    fields_ref,
     rhs_ref,
     diag_ref,
     off_ref,
@@ -111,14 +110,27 @@
     edge_sem,
     sum_send_sem,
     sum_sem,
+    here_sem,
 ):
     here = tuple(lax.axis_index(axis) for axis in AXES)
     index_x, index_y, index_z = here
 
+    places = {}
+
     def at(steps):
-        return tuple(
-            wrapped(here[i], steps[i], sizes[i]) if steps[i] else here[i] for i in range(3)
-        )
+        for axis in range(3):
+            step = steps[axis] % sizes[axis]
+            if (axis, step) not in places:
+                moved_on = here[axis] + step
+                places[axis, step] = (
+                    jnp.where(moved_on >= sizes[axis], moved_on - sizes[axis], moved_on)
+                    if step
+                    else here[axis]
+                )
+        return tuple(places[axis, steps[axis] % sizes[axis]] for axis in range(3))
+
+    def signal(semaphore, steps):
+        pl.semaphore_signal(semaphore, inc=1, device_id=at(steps), device_id_type=MESH)
 
     lines = []
     for axis in (0, 1, 2):
@@ -128,18 +140,6 @@
             steps[axis] = step
             line.append(tuple(steps))
         lines.append(line)
-
-    partners = {tuple(s % n for s, n in zip(steps, sizes)) for line in lines for steps in line}
-    partners |= {
-        tuple(s % n for s, n in zip((dx, dy, dz), sizes))
-        for dx in (-1, 0, 1)
-        for dy, dz in SIDES
-        if (dx, dy, dz) != (0, 0, 0)
-    }
-    partners = sorted(partners)
-    barrier = pltpu.get_barrier_semaphore()
-    for steps in partners:
-        pl.semaphore_signal(barrier, inc=1, device_id=at(steps), device_id_type=MESH)
 
     loads = [
         pltpu.make_async_copy(source, target, load_sem.at[i])
@@ -155,7 +155,13 @@
             )
         )
     ]
-    for load in loads:
+    loads[0].start()
+
+    barrier = pltpu.get_barrier_semaphore()
+    for steps in NEIGHBOURS:
+        signal(barrier, steps)
+
+    for load in loads[1:]:
         load.start()
 
     lane = lax.broadcasted_iota(jnp.int32, (NODES, LANES), 1)
@@ -221,29 +227,26 @@
             outgoing[turn, k, pl.ds(ROWS, NODES), :] = last_tile(message)
 
     def edge_row(dx, k):
-        return (16 if k == 8 else 8 * 0 + k) + ((1 if k == 8 else 8) if dx < 0 else 0)
+        row_before = 16 if k == 8 else k
+        return row_before + (1 if k == 8 else 8) * (dx < 0)
 
     def send(turn):
-        for k, (dy, dz) in enumerate(SIDES):
-            for dx in (-1, 1):
-                source = ROWS + NODES - 1 if dx > 0 else 0
-                pltpu.make_async_remote_copy(
-                    src_ref=outgoing.at[turn, k, pl.ds(source, 1)],
-                    dst_ref=edges.at[turn, pl.ds(edge_row(dx, k), 1)],
-                    send_sem=send_sem.at[turn, 1],
-                    recv_sem=edge_sem.at[turn],
-                    device_id=at((dx, dy, dz)),
-                    device_id_type=MESH,
-                ).start()
-            if k < 8:
-                pltpu.make_async_remote_copy(
-                    src_ref=outgoing.at[turn, k, pl.ds(0, ROWS)],
-                    dst_ref=fields.at[turn, pl.ds(k * ROWS, ROWS)],
-                    send_sem=send_sem.at[turn, 0],
-                    recv_sem=field_sem.at[turn],
-                    device_id=at((0, dy, dz)),
-                    device_id_type=MESH,
-                ).start()
+        for steps in NEIGHBOURS:
+            dx, k = steps[0], SIDES.index(steps[1:])
+            if dx:
+                source, count = (ROWS + NODES - 1 if dx > 0 else 0), 1
+                target, row_to, sem, kind = edges, edge_row(dx, k), edge_sem, 1
+            else:
+                source, count = 0, ROWS
+                target, row_to, sem, kind = fields, k * ROWS, field_sem, 0
+            pltpu.make_async_remote_copy(
+                src_ref=outgoing.at[turn, k, pl.ds(source, count)],
+                dst_ref=target.at[turn, pl.ds(row_to, count)],
+                send_sem=send_sem.at[turn, kind],
+                recv_sem=sem.at[turn],
+                device_id=at(steps),
+                device_id_type=MESH,
+            ).start()
 
     def wait_bytes(ref, sem):
         pltpu.make_async_copy(ref, ref, sem).wait()
@@ -328,6 +331,8 @@
     ]
     base = joined(raw)
     pack(0, base)
+    pl.semaphore_wait(barrier, len(NEIGHBOURS))
+    send(0)
     for load in loads[1:]:
         load.wait()
     for matrix, terms in ((forward_ref, forward_terms), (backward_ref, backward_terms)):
@@ -337,9 +342,28 @@
         terms[0:depth, :] = high
         terms[depth : 2 * depth, :] = high
         terms[2 * depth : 3 * depth, :] = (values - high.astype(F32)).astype(BF16)
-    pl.semaphore_wait(barrier, len(partners))
-    send(0)
     base = receive(0, base)
+
+    rounds = []
+    reach = 2
+    while any(reach < size // 2 for size in sizes):
+        rounds.append([(axis, reach) for axis in range(3) if reach < sizes[axis] // 2])
+        reach *= 2
+
+    def announce(turn):
+        for axis, reach in rounds[turn]:
+            for way in (0, 1):
+                steps = [0, 0, 0]
+                steps[axis] = reach if way else -reach
+                signal(here_sem.at[turn, axis, way], steps)
+
+    def hear(turn):
+        for axis, unused_reach in rounds[turn]:
+            for way in (0, 1):
+                pl.semaphore_wait(here_sem.at[turn, axis, way], 1)
+
+    if rounds:
+        announce(0)
 
     unused, flux = fluxes(base)
     first_raw = image_of(flux, mass_times(base))
@@ -348,6 +372,10 @@
     send(1)
     moment0 = dot(base, raw)
     moment1 = dot(base, first_raw)
+    for turn in range(len(rounds)):
+        hear(turn)
+        if turn + 1 < len(rounds):
+            announce(turn + 1)
     first = receive(1, first)
 
     moment2 = dot(first, first_raw)
@@ -399,17 +427,25 @@
             pltpu.roll(out[2], NODES - 2, 0),
         ]
 
+    def keep_grid(which, tiles):
+        for slot in range(SLOTS):
+            count = min(NODES, PLANES_X - slot * NODES)
+            fields_ref[which, pl.ds(slot * NODES, count), :] = tiles[slot][:count, :PLANES_YZ]
+
     start_line(0, total)
     second = joined(image_of(flux, mass_part))
     pack(2, second)
     send(2)
-    base_grid = packed_grid(base)
-    first_grid = packed_grid(first)
+    keep_grid(0, packed_grid(base))
+    keep_grid(1, packed_grid(first))
     total = finish_line(0, total)
     start_line(1, total)
-    second_grid = packed_grid(receive(2, second))
+    keep_grid(2, packed_grid(receive(2, second)))
     total = finish_line(1, total)
     start_line(2, total)
+    for turn in range(3):
+        wait_bytes(edges.at[turn, pl.ds(0, 18)], send_sem.at[turn, 1])
+        wait_bytes(fields.at[turn], send_sem.at[turn, 0])
     total = finish_line(2, total)
 
     group = lax.broadcasted_iota(jnp.int32, (1, LANES), 1) // 32
@@ -421,17 +457,9 @@
     alpha1 = alpha0 * (gain - 1.0) / (alpha0 * (alpha0 * (m3 / m1)) - gain * gain)
     scale0 = alpha0 + alpha1 * gain
     scale1 = alpha0 * alpha1
-    for slot in range(SLOTS):
-        count = min(NODES, PLANES_X - slot * NODES)
-        at_slot = pl.ds(slot * NODES, count)
-        iterate = scale0 * base_grid[slot] - scale1 * first_grid[slot]
-        rest = base_grid[slot] - scale0 * first_grid[slot] + scale1 * second_grid[slot]
-        solution_ref[at_slot, :] = iterate[:count, :PLANES_YZ]
-        residual_ref[at_slot, :] = rest[:count, :PLANES_YZ]
-
-    for turn in range(3):
-        wait_bytes(edges.at[turn, pl.ds(0, 18)], send_sem.at[turn, 1])
-        wait_bytes(fields.at[turn], send_sem.at[turn, 0])
+    fields_ref[3] = jnp.broadcast_to(scale0, (PLANES_X, PLANES_YZ))
+    fields_ref[4] = jnp.broadcast_to(scale1, (PLANES_X, PLANES_YZ))
+
     for axis in range(3):
         wait_bytes(sums_in.at[axis, pl.ds(0, len(lines[axis]))], sum_send_sem.at[axis])
 
@@ -439,14 +467,12 @@
 def local(sizes, rhs_local, geom_diag, geom_off, mass_coef, elem_counts):
     forward, backward, radial = tables()
     hbm = pl.BlockSpec(memory_space=pltpu.HBM)
-    vmem = pl.BlockSpec(memory_space=pltpu.VMEM)
-    out = jax.ShapeDtypeStruct((PLANES_X, PLANES_YZ), F32)
-    return pl.pallas_call(
+    base, first, second, scale0, scale1 = pl.pallas_call(
         functools.partial(kernel, sizes),
         name="cg",
-        out_shape=(out, out),
+        out_shape=jax.ShapeDtypeStruct((5, PLANES_X, PLANES_YZ), F32),
         in_specs=[pl.BlockSpec(memory_space=pltpu.SMEM)] + [hbm] * 7,
-        out_specs=(vmem, vmem),
+        out_specs=pl.BlockSpec(memory_space=pltpu.VMEM),
         scratch_shapes=[
             pltpu.VMEM((ROWS, LANES), F32),
             pltpu.VMEM((3, ROWS, LANES), F32),
@@ -468,6 +494,7 @@
             pltpu.SemaphoreType.DMA((3,)),
             pltpu.SemaphoreType.DMA((3,)),
             pltpu.SemaphoreType.DMA((3,)),
+            pltpu.SemaphoreType.REGULAR((4, 3, 2)),
         ],
         compiler_params=pltpu.CompilerParams(
             collective_id=0, has_side_effects=True, vmem_limit_bytes=16 * 1024 * 1024
@@ -487,6 +514,7 @@
             )
         ),
     )
+    return scale0 * base - scale1 * first, base - scale0 * first + scale1 * second
 
 
 def solution(mesh):

time: 52.5 us -> 49.4 us (0.941)
  Pallas kernels: 49.8 us -> 47.3 us
  local copies, waits for them, and re-layouts: 1.2 us -> 0 us
  other arithmetic: 0 us -> 0.61 us
    pallas_call x1, Pallas kernels: 49.8 us -> 47.3 us  [local(): pl.pallas_call(functools.partial(kernel, sizes), name='cg', out_shape=jax...]
    unnamed x2 -> x0, local copies, waits for them, and re-layouts: 1.2 us -> none
    add x0 -> x1, other arithmetic: none -> 0.61 us  [local(): base - scale0 * first + scale1 * second]
where the time goes in v2:
time: 49.4 us; the launch traced here: 49.2 us
  Pallas kernels  47.3 us (96%)
  between operations  1.29 us (3%)
  other arithmetic  0.61 us (1%)
    pallas_call x1, Pallas kernels, local(): pl.pallas_call(functools.partial(kernel, sizes), name='cg', out_shape=jax...  47.3 us

profile of v2, /device:TPU:1, one launch (start us, length us, event | category | flops | bytes accessed | tf_op | source)
XLA Modules:
  0.0 49.2 jit_solution(7195420413600894681)
XLA Ops:
  1.3 47.3 %cg.1 = f32[5,22,120]{2,1,0:T(8,128)S(1)} custom-call(s32[1]{0:T(128)S(6)} %copy.10.counts_ref, f32[24,128]{1,0:T(8,128)} %rhs_hbm.1, f32[3,24,128]{2,1,0:T(8,128)} %diag_hbm.1, f32[3,24,128]{2,1,0:T(8,128)} %off_hbm.1, f32[24,128]{1,0:T(8,128)} %mass_hbm.1, f32[128,256]{1,0:T(8,128)} %constant.6.clone.forward_hbm, f32[256,128]{1,0:T(8,128)} %constant.7.clone.backward_hbm, ...), custom_call_target="tpu_custom_call" | custom-call | tf_op jit(solution)/shard_map/cg/pallas_call | solution.py:470
  48.6 0.6 %fusion = (f32[22,120]{1,0:T(8,128)}, f32[22,120]{1,0:T(8,128)}) fusion(f32[5,22,120]{2,1,0:T(8,128)S(1)} %cg.1), kind=kLoop, calls=%fused_computation.1 | loop fusion | flops 18480 | bytes 73920 | tf_op jit(solution)/shard_map/add | solution.py:517

commit v3 on v2

--- a/solution.py
+++ b/solution.py
@@ -132,14 +132,23 @@
     def signal(semaphore, steps):
         pl.semaphore_signal(semaphore, inc=1, device_id=at(steps), device_id_type=MESH)
 
-    lines = []
-    for axis in (0, 1, 2):
-        line = []
-        for step in range(1, sizes[axis]):
-            steps = [0, 0, 0]
-            steps[axis] = step
-            line.append(tuple(steps))
-        lines.append(line)
+    def distance(steps):
+        around = [min(step % size, -step % size) for step, size in zip(steps, sizes)]
+        return around[0] + around[1] / 2 + around[2]
+
+    groups = [
+        sorted(((step, 0, 0) for step in range(1, sizes[0])), key=distance, reverse=True),
+        sorted(
+            (
+                (0, step_y, step_z)
+                for step_y in range(sizes[1])
+                for step_z in range(sizes[2])
+                if step_y or step_z
+            ),
+            key=distance,
+            reverse=True,
+        ),
+    ]
 
     loads = [
         pltpu.make_async_copy(source, target, load_sem.at[i])
@@ -397,9 +406,9 @@
     )
     total = jnp.sum(pairs, axis=0, keepdims=True)
 
-    def start_line(axis, value):
+    def start_group(axis, value):
         sums_out[axis, 0:1, :] = value
-        for k, steps in enumerate(lines[axis]):
+        for k, steps in enumerate(groups[axis]):
             pltpu.make_async_remote_copy(
                 src_ref=sums_out.at[axis, pl.ds(0, 1)],
                 dst_ref=sums_in.at[axis, pl.ds(k, 1)],
@@ -409,8 +418,8 @@
                 device_id_type=MESH,
             ).start()
 
-    def finish_line(axis, value):
-        count = len(lines[axis])
+    def finish_group(axis, value):
+        count = len(groups[axis])
         wait_bytes(sums_in.at[axis, pl.ds(0, count)], sum_sem.at[axis])
         return value + jnp.sum(sums_in[axis, 0:count, :], axis=0, keepdims=True)
 
@@ -432,21 +441,19 @@
             count = min(NODES, PLANES_X - slot * NODES)
             fields_ref[which, pl.ds(slot * NODES, count), :] = tiles[slot][:count, :PLANES_YZ]
 
-    start_line(0, total)
+    start_group(0, total)
     second = joined(image_of(flux, mass_part))
     pack(2, second)
     send(2)
     keep_grid(0, packed_grid(base))
     keep_grid(1, packed_grid(first))
-    total = finish_line(0, total)
-    start_line(1, total)
+    total = finish_group(0, total)
+    start_group(1, total)
     keep_grid(2, packed_grid(receive(2, second)))
-    total = finish_line(1, total)
-    start_line(2, total)
     for turn in range(3):
         wait_bytes(edges.at[turn, pl.ds(0, 18)], send_sem.at[turn, 1])
         wait_bytes(fields.at[turn], send_sem.at[turn, 0])
-    total = finish_line(2, total)
+    total = finish_group(1, total)
 
     group = lax.broadcasted_iota(jnp.int32, (1, LANES), 1) // 32
     m2, m0, m3, m1 = (
@@ -460,8 +467,8 @@
     fields_ref[3] = jnp.broadcast_to(scale0, (PLANES_X, PLANES_YZ))
     fields_ref[4] = jnp.broadcast_to(scale1, (PLANES_X, PLANES_YZ))
 
-    for axis in range(3):
-        wait_bytes(sums_in.at[axis, pl.ds(0, len(lines[axis]))], sum_send_sem.at[axis])
+    for axis in range(2):
+        wait_bytes(sums_in.at[axis, pl.ds(0, len(groups[axis]))], sum_send_sem.at[axis])
 
 
 def local(sizes, rhs_local, geom_diag, geom_off, mass_coef, elem_counts):
@@ -486,8 +493,8 @@
             pltpu.VMEM((3, 9, ROWS + NODES, LANES), F32),
             pltpu.VMEM((3, 8 * ROWS, LANES), F32),
             pltpu.VMEM((3, 24, LANES), F32),
-            pltpu.VMEM((3, 8, LANES), F32),
-            pltpu.VMEM((3, 16, LANES), F32),
+            pltpu.VMEM((2, 8, LANES), F32),
+            pltpu.VMEM((2, 64, LANES), F32),
             pltpu.SemaphoreType.DMA((7,)),
             pltpu.SemaphoreType.DMA((3, 2)),
             pltpu.SemaphoreType.DMA((3,)),

time: 49.4 us -> 48.2 us (0.976)
  Pallas kernels: 47.3 us -> 46.1 us
    pallas_call x1, Pallas kernels: 47.3 us -> 46.1 us  [local(): pl.pallas_call(functools.partial(kernel, sizes), name='cg', out_shape=jax...]
where the time goes in v3:
time: 48.2 us; the launch traced here: 48 us
  Pallas kernels  46.1 us (96%)
  between operations  1.29 us (3%)
  other arithmetic  0.61 us (1%)
    pallas_call x1, Pallas kernels, local(): pl.pallas_call(functools.partial(kernel, sizes), name='cg', out_shape=jax...  46.1 us

profile of v3, /device:TPU:1, one launch (start us, length us, event | category | flops | bytes accessed | tf_op | source)
XLA Modules:
  0.0 48.0 jit_solution(7615817073720778530)
XLA Ops:
  1.3 46.1 %cg.1 = f32[5,22,120]{2,1,0:T(8,128)S(1)} custom-call(s32[1]{0:T(128)S(6)} %copy.10.counts_ref, f32[24,128]{1,0:T(8,128)} %rhs_hbm.1, f32[3,24,128]{2,1,0:T(8,128)} %diag_hbm.1, f32[3,24,128]{2,1,0:T(8,128)} %off_hbm.1, f32[24,128]{1,0:T(8,128)} %mass_hbm.1, f32[128,256]{1,0:T(8,128)} %constant.6.clone.forward_hbm, f32[256,128]{1,0:T(8,128)} %constant.7.clone.backward_hbm, ...), custom_call_target="tpu_custom_call" | custom-call | tf_op jit(solution)/shard_map/cg/pallas_call | solution.py:477
  47.3 0.6 %fusion = (f32[22,120]{1,0:T(8,128)}, f32[22,120]{1,0:T(8,128)}) fusion(f32[5,22,120]{2,1,0:T(8,128)S(1)} %cg.1), kind=kLoop, calls=%fused_computation.1 | loop fusion | flops 18480 | bytes 73920 | tf_op jit(solution)/shard_map/add | solution.py:524

commit v4 on v3

--- a/solution.py
+++ b/solution.py
@@ -127,7 +127,10 @@
                     if step
                     else here[axis]
                 )
-        return tuple(places[axis, steps[axis] % sizes[axis]] for axis in range(3))
+        place = [places[axis, steps[axis] % sizes[axis]] for axis in range(3)]
+        if len(steps) == 4:
+            place[1] = index_y + 1 - 2 * lax.rem(index_y, 2)
+        return tuple(place)
 
     def signal(semaphore, steps):
         pl.semaphore_signal(semaphore, inc=1, device_id=at(steps), device_id_type=MESH)
@@ -137,11 +140,16 @@
         return around[0] + around[1] / 2 + around[2]
 
     groups = [
-        sorted(((step, 0, 0) for step in range(1, sizes[0])), key=distance, reverse=True),
+        sorted(
+            [(step, 0, 0) for step in range(1, sizes[0])]
+            + [(step, 0, 0, 1) for step in range(sizes[0])],
+            key=distance,
+            reverse=True,
+        ),
         sorted(
             (
                 (0, step_y, step_z)
-                for step_y in range(sizes[1])
+                for step_y in range(0, sizes[1], 2)
                 for step_z in range(sizes[2])
                 if step_y or step_z
             ),
@@ -166,8 +174,15 @@
     ]
     loads[0].start()
 
+    taken = {tuple(step % size for step, size in zip(steps, sizes)) for steps in NEIGHBOURS}
+    greeted = NEIGHBOURS + [
+        (0, step_y, step_z)
+        for step_y in (-1, 0, 1)
+        for step_z in range(2, sizes[2] - 1)
+        if (0, step_y % sizes[1], step_z) not in taken
+    ]
     barrier = pltpu.get_barrier_semaphore()
-    for steps in NEIGHBOURS:
+    for steps in greeted:
         signal(barrier, steps)
 
     for load in loads[1:]:
@@ -340,8 +355,28 @@
     ]
     base = joined(raw)
     pack(0, base)
-    pl.semaphore_wait(barrier, len(NEIGHBOURS))
+    pl.semaphore_wait(barrier, len(greeted))
     send(0)
+    rounds = []
+    reach = 1
+    while any(reach < size // 2 for size in sizes[:2]):
+        rounds.append([(axis, reach) for axis in (0, 1) if reach < sizes[axis] // 2])
+        reach *= 2
+
+    def announce(turn):
+        for axis, reach in rounds[turn]:
+            for way in (0, 1):
+                steps = [0, 0, 0]
+                steps[axis] = reach if way else -reach
+                signal(here_sem.at[turn, axis, way], steps)
+
+    def hear(turn):
+        for axis, unused_reach in rounds[turn]:
+            for way in (0, 1):
+                pl.semaphore_wait(here_sem.at[turn, axis, way], 1)
+
+    if rounds:
+        announce(0)
     for load in loads[1:]:
         load.wait()
     for matrix, terms in ((forward_ref, forward_terms), (backward_ref, backward_terms)):
@@ -351,28 +386,10 @@
         terms[0:depth, :] = high
         terms[depth : 2 * depth, :] = high
         terms[2 * depth : 3 * depth, :] = (values - high.astype(F32)).astype(BF16)
+    for turn in range(len(rounds) - 1):
+        hear(turn)
+        announce(turn + 1)
     base = receive(0, base)
-
-    rounds = []
-    reach = 2
-    while any(reach < size // 2 for size in sizes):
-        rounds.append([(axis, reach) for axis in range(3) if reach < sizes[axis] // 2])
-        reach *= 2
-
-    def announce(turn):
-        for axis, reach in rounds[turn]:
-            for way in (0, 1):
-                steps = [0, 0, 0]
-                steps[axis] = reach if way else -reach
-                signal(here_sem.at[turn, axis, way], steps)
-
-    def hear(turn):
-        for axis, unused_reach in rounds[turn]:
-            for way in (0, 1):
-                pl.semaphore_wait(here_sem.at[turn, axis, way], 1)
-
-    if rounds:
-        announce(0)
 
     unused, flux = fluxes(base)
     first_raw = image_of(flux, mass_times(base))
@@ -381,10 +398,6 @@
     send(1)
     moment0 = dot(base, raw)
     moment1 = dot(base, first_raw)
-    for turn in range(len(rounds)):
-        hear(turn)
-        if turn + 1 < len(rounds):
-            announce(turn + 1)
     first = receive(1, first)
 
     moment2 = dot(first, first_raw)
@@ -441,6 +454,8 @@
             count = min(NODES, PLANES_X - slot * NODES)
             fields_ref[which, pl.ds(slot * NODES, count), :] = tiles[slot][:count, :PLANES_YZ]
 
+    if rounds:
+        hear(len(rounds) - 1)
     start_group(0, total)
     second = joined(image_of(flux, mass_part))
     pack(2, second)

time: 48.2 us -> 45.3 us (0.940)
  Pallas kernels: 46.1 us -> 43.2 us
    pallas_call x1, Pallas kernels: 46.1 us -> 43.2 us  [local(): pl.pallas_call(functools.partial(kernel, sizes), name='cg', out_shape=jax...]
where the time goes in v4:
time: 45.3 us; the launch traced here: 45.1 us
  Pallas kernels  43.2 us (95%)
  between operations  1.29 us (3%)
  other arithmetic  0.61 us (1%)
    pallas_call x1, Pallas kernels, local(): pl.pallas_call(functools.partial(kernel, sizes), name='cg', out_shape=jax...  43.2 us

profile of v4, /device:TPU:1, one launch (start us, length us, event | category | flops | bytes accessed | tf_op | source)
XLA Modules:
  0.0 45.1 jit_solution(8320497628063958269)
XLA Ops:
  1.3 43.2 %cg.1 = f32[5,22,120]{2,1,0:T(8,128)S(1)} custom-call(s32[1]{0:T(128)S(6)} %copy.10.counts_ref, f32[24,128]{1,0:T(8,128)} %rhs_hbm.1, f32[3,24,128]{2,1,0:T(8,128)} %diag_hbm.1, f32[3,24,128]{2,1,0:T(8,128)} %off_hbm.1, f32[24,128]{1,0:T(8,128)} %mass_hbm.1, f32[128,256]{1,0:T(8,128)} %constant.6.clone.forward_hbm, f32[256,128]{1,0:T(8,128)} %constant.7.clone.backward_hbm, ...), custom_call_target="tpu_custom_call" | custom-call | tf_op jit(solution)/shard_map/cg/pallas_call | solution.py:492
  44.5 0.6 %fusion = (f32[22,120]{1,0:T(8,128)}, f32[22,120]{1,0:T(8,128)}) fusion(f32[5,22,120]{2,1,0:T(8,128)S(1)} %cg.1), kind=kLoop, calls=%fused_computation.1 | loop fusion | flops 18480 | bytes 73920 | tf_op jit(solution)/shard_map/add | solution.py:539

commit v5 on v4

--- a/solution.py
+++ b/solution.py
@@ -129,7 +129,7 @@
                 )
         place = [places[axis, steps[axis] % sizes[axis]] for axis in range(3)]
         if len(steps) == 4:
-            place[1] = index_y + 1 - 2 * lax.rem(index_y, 2)
+            place[1] = place[1] + 1 - 2 * lax.rem(place[1], 2)
         return tuple(place)
 
     def signal(semaphore, steps):
@@ -276,12 +276,7 @@
         pltpu.make_async_copy(ref, ref, sem).wait()
 
     def receive(turn, tiles):
-        wait_bytes(edges.at[turn, pl.ds(0, 18)], edge_sem.at[turn])
         wait_bytes(fields.at[turn], field_sem.at[turn])
-        before = jnp.sum(edges[turn, 0:8, :], axis=0, keepdims=True) + edges[turn, 16:17, :]
-        after = jnp.sum(edges[turn, 8:16, :], axis=0, keepdims=True) + edges[turn, 17:18, :]
-        before = jnp.where((row == 0) & (index_x > 0), before, zero)
-        after = jnp.where((row == NODES - 1) & (index_x < sizes[0] - 1), after, zero)
         out = []
         for slot in range(SLOTS):
             parts = [
@@ -290,11 +285,16 @@
             total = ((parts[0] + parts[1]) + (parts[2] + parts[3])) + (
                 (parts[4] + parts[5]) + (parts[6] + parts[7])
             )
-            if slot == 0:
-                total = total + before
+            out.append(tiles[slot] + total)
+        wait_bytes(edges.at[turn, pl.ds(0, 18)], edge_sem.at[turn])
+        before = jnp.sum(edges[turn, 0:8, :], axis=0, keepdims=True) + edges[turn, 16:17, :]
+        after = jnp.sum(edges[turn, 8:16, :], axis=0, keepdims=True) + edges[turn, 17:18, :]
+        before = jnp.where((row == 0) & (index_x > 0), before, zero)
+        after = jnp.where((row == NODES - 1) & (index_x < sizes[0] - 1), after, zero)
+        for slot in range(SLOTS):
             is_last = live[slot] & jnp.logical_not(live[slot + 1]) if slot + 1 < SLOTS else live[slot]
-            total = total + jnp.where(is_last, after, zero)
-            out.append(tiles[slot] + total)
+            extra = jnp.where(is_last, after, zero)
+            out[slot] = out[slot] + (extra + before if slot == 0 else extra)
         return out
 
     def three_terms(values):

time: 45.3 us -> 45.3 us (level)
  no operation moved by 1% of the time
where the time goes in v5:
time: 45.3 us; the launch traced here: 45.1 us
  Pallas kernels  43.2 us (95%)
  between operations  1.29 us (3%)
  other arithmetic  0.61 us (1%)
    pallas_call x1, Pallas kernels, local(): pl.pallas_call(functools.partial(kernel, sizes), name='cg', out_shape=jax...  43.2 us

profile of v5, /device:TPU:1, one launch (start us, length us, event | category | flops | bytes accessed | tf_op | source)
XLA Modules:
  0.0 45.1 jit_solution(8746645920448360575)
XLA Ops:
  1.3 43.2 %cg.1 = f32[5,22,120]{2,1,0:T(8,128)S(1)} custom-call(s32[1]{0:T(128)S(6)} %copy.10.counts_ref, f32[24,128]{1,0:T(8,128)} %rhs_hbm.1, f32[3,24,128]{2,1,0:T(8,128)} %diag_hbm.1, f32[3,24,128]{2,1,0:T(8,128)} %off_hbm.1, f32[24,128]{1,0:T(8,128)} %mass_hbm.1, f32[128,256]{1,0:T(8,128)} %constant.6.clone.forward_hbm, f32[256,128]{1,0:T(8,128)} %constant.7.clone.backward_hbm, ...), custom_call_target="tpu_custom_call" | custom-call | tf_op jit(solution)/shard_map/cg/pallas_call | solution.py:492
  44.5 0.6 %fusion = (f32[22,120]{1,0:T(8,128)}, f32[22,120]{1,0:T(8,128)}) fusion(f32[5,22,120]{2,1,0:T(8,128)S(1)} %cg.1), kind=kLoop, calls=%fused_computation.1 | loop fusion | flops 18480 | bytes 73920 | tf_op jit(solution)/shard_map/add | solution.py:539
